TPU v7x, 512 devices: a whole 4x4x16 slice. The times are simulated.
512 devices in a mesh: neuron: 32 (over z_lo, x, core), pos: 4 (over y), trial: 4 (over z_hi).
Axes of the slice: x: 4, y: 4, z: 16 (z_hi: 4, z_lo: 4; z = z_hi * 4 + z_lo), core: 2. Of those that a mesh axis runs over, the one named last changes fastest.
Arguments:
- counts: int32 [64, 256, 16384], P('trial', 'pos', 'neuron'), may hold values from 0 to 7
- neuron_factors: float32 [16, 16384], P(None, 'neuron'), may hold values from 0.2 to 1
- pos_factors: float32 [16, 256], P(None, 'pos'), may hold values from 0.2 to 1
- trial_factors: float32 [16, 64], P(None, 'trial'), may hold values from 0.2 to 1
Outputs:
- grad_neuron: float32 [16, 16384], replicated
- grad_pos: float32 [16, 256], replicated
- grad_trial: float32 [16, 64], replicated
All inputs are finite; a program needn't handle non-finite values.
Results may differ from a plain program's by a relative error of at most 0.0001.
Values sent between devices are 32-bit elements; how exact they have to be, the bound alone decides.
A program may use at most 64 MiB of HBM per device.

v0:
```python
import jax
import jax.numpy as jnp
from jax import lax
from jax.sharding import PartitionSpec as P


def body(counts, neuron_factors, pos_factors, trial_factors):
    highest = lax.Precision.HIGHEST
    k_dev, j_dev, i_dev = counts.shape
    ranks = neuron_factors.shape[0]
    neurons_total = i_dev * lax.axis_size("neuron")
    pos_total = j_dev * lax.axis_size("pos")
    trials_total = k_dev * lax.axis_size("trial")
    khatri = (trial_factors[:, :, None] * pos_factors[:, None, :]).reshape(ranks, k_dev * j_dev)
    model = jnp.dot(khatri.T, neuron_factors, precision=highest)
    ratio = 1.0 - counts.reshape(k_dev * j_dev, i_dev).astype(jnp.float32) / model
    part_a = jnp.dot(khatri, ratio, precision=highest) / (pos_total * trials_total)
    projected = jnp.dot(ratio, neuron_factors.T, precision=highest).reshape(k_dev, j_dev, ranks)
    part_b = jnp.einsum("kjr,rk->rj", projected, trial_factors, precision=highest) / (
        neurons_total * trials_total
    )
    part_c = jnp.einsum("kjr,rj->rk", projected, pos_factors, precision=highest) / (
        neurons_total * pos_total
    )
    summed_a = lax.psum(part_a, ("pos", "trial"))
    grad_neuron = lax.all_gather(summed_a, "neuron", axis=1, tiled=True)
    summed_b = lax.psum(part_b, ("neuron", "trial"))
    grad_pos = lax.all_gather(summed_b, "pos", axis=1, tiled=True)
    summed_c = lax.psum(part_c, ("neuron", "pos"))
    grad_trial = lax.all_gather(summed_c, "trial", axis=1, tiled=True)
    return (grad_neuron, grad_pos, grad_trial)


def solution(mesh):
    placed = (P("trial", "pos", "neuron"), P(None, "neuron"), P(None, "pos"), P(None, "trial"))
    return jax.shard_map(
        body, mesh=mesh, in_specs=placed, out_specs=(P(), P(), P()), check_vma=False
    )
```

profile of v0, /device:TPU:32, one launch (start us, length us, event | category | flops | bytes accessed | tf_op | source)
XLA Modules:
  0.0 824.2 jit_solution(414768877686551168)
XLA Ops:
  7.2 0.0 copy-start
  7.2 0.0 all-gather.3.cloned.1.call-start
  7.2 0.8 broadcast_multiply_fusion
  8.0 0.1 mul.20
  8.1 0.0 copy-done
  8.1 3.6 fusion
  11.8 0.0 copy-start.1
  11.8 0.0 copy-start.2
  11.8 1.1 convolution_multiply_fusion
  12.9 104.0 %psum.21 = f32[16,512]{1,0:T(8,128)} all-reduce(f32[16,512]{1,0:T(8,128)S(1)} %convolution_multiply_fusion), channel_id=1, replica_groups=mesh['neuron'=32,'pos'=4,'trial'=4] {'pos','trial'}, use_global_device_ids=true, to_apply=%region_0.0 | all-reduce | flops 8192 | bytes 65536 | tf_op jit(solution)/shard_map/psum | solution.py:25
  116.9 0.0 all-gather.3.cloned.1.call-update
  116.9 1.9 fusion.1
  118.8 0.1 reshape.17
  118.8 0.0 copy-done.1
  118.9 0.3 fusion.3
  119.2 0.1 copy.13
  119.3 279.8 %psum.23 = f32[16,16]{0,1:T(8,128)S(1)} all-reduce(f32[16,16]{0,1:T(8,128)S(1)} %bitcast_multiply_fusion), channel_id=1, replica_groups=mesh['neuron'=32,'pos'=4,'trial'=4] {'neuron','pos'}, use_global_device_ids=true, to_apply=%region_2.0 | all-reduce | flops 256 | bytes 2048 | tf_op jit(solution)/shard_map/psum | solution.py:29
  399.1 17.3 %all_gather.11 = f32[16,64]{0,1:T(8,128)S(1)} all-gather(f32[16,16]{0,1:T(8,128)S(1)} %psum.23), channel_id=1, replica_groups=mesh['neuron'=32,'pos'=4,'trial'=4] {'trial'}, dimensions={1}, use_global_device_ids=true | all-gather | bytes 5120 | tf_op jit(solution)/shard_map/all_gather | solution.py:30
  416.4 0.7 copy.9
  417.1 0.0 copy-done.2
  417.1 0.3 fusion.2
  417.4 385.1 %psum.22 = f32[16,64]{1,0:T(8,128)S(1)} all-reduce(f32[16,64]{1,0:T(8,128)S(1)} %broadcast_multiply_fusion.1), channel_id=1, replica_groups=mesh['neuron'=32,'pos'=4,'trial'=4] {'neuron','trial'}, use_global_device_ids=true, to_apply=%region_1.0 | all-reduce | flops 1024 | bytes 8192 | tf_op jit(solution)/shard_map/psum | solution.py:27
  802.4 11.9 %all-gather = f32[4,64,16]{1,2,0:T(8,128)S(1)} all-gather(f32[1,64,16]{1,2,0:T(8,128)S(1)} %bitcast.35), channel_id=1, replica_groups=mesh['neuron'=32,'pos'=4,'trial'=4] {'pos'}, dimensions={0}, use_global_device_ids=true | all-gather | bytes 20480 | tf_op jit(solution)/shard_map/all_gather | solution.py:28
  814.4 0.7 reshape.19
  815.0 0.0 all-gather.3.cloned.1.call-done
  815.0 2.3 copy.15
  (3 shorter events, 0.0 us)
Async XLA Ops:
  7.2 1.0 copy-start
  7.2 807.9 %all-gather.3.cloned.1.call-start = ((), (), s32[]{:S(2)}) async-start(), calls=%async_computation | async-start | bytes 1081344 | tf_op jit(solution)/shard_map/all_gather | solution.py:26
  11.8 107.1 %copy-start.1 = (f32[16,64]{1,0:T(8,128)S(1)}, f32[16,64]{1,0:T(8,128)}, u32[]{:S(2)}) copy-start(f32[16,64]{1,0:T(8,128)} %param.6) | copy-start | bytes 12292
  11.8 405.3 %copy-start.2 = (f32[16,16]{1,0:T(8,128)S(1)}, f32[16,16]{1,0:T(8,128)}, u32[]{:S(2)}) copy-start(f32[16,16]{1,0:T(8,128)} %param.7) | copy-start | bytes 3076
Sparse Core Ops, SparseCore 0:
  117.0 55.4 all-gather.2
where the time goes:
time: 824 us
  blocking collectives  798 us (97%)
  between operations  14.1 us (2%)
    psum x1, blocking collectives, body(): summed_b = lax.psum(part_b, ('neuron', 'trial'))  385 us
    psum x1, blocking collectives, body(): summed_c = lax.psum(part_c, ('neuron', 'pos'))  280 us
    psum x1, blocking collectives, body(): summed_a = lax.psum(part_a, ('pos', 'trial'))  104 us
    all_gather x1, blocking collectives, body(): grad_trial = lax.all_gather(summed_c, 'trial', axis=1, tiled=True)  17.3 us
  transfers between devices with their start and end apart: 1, of which 0 were waited for; matrix products, arithmetic and copies ran while one was open for 0% of the time, Pallas kernels for 0%

commit v1 on v0

v1 whole, which is shorter than its diff:
```python
import jax
import jax.numpy as jnp
from jax import lax
from jax.experimental import pallas as pl
from jax.experimental.pallas import tpu as pltpu
from jax.sharding import PartitionSpec as P

MESH = pl.DeviceIdType.MESH
RING = (0, 1, -1, 2)
LANES = 128


def split(value):
    high = value.astype(jnp.bfloat16).astype(jnp.float32)
    return high, value - high


def kernel(
    counts_hbm, nf_ref, pf_ref, tf_ref, gn_ref, gp_ref, gt_ref,
    counts, stage, proj, part_a, sum_a, part_v, sum_v, mean_v, far_v, final,
    a1, a2, v1, v2, v3, other,
    counts_sem, a1_s, a1_r, a2_s, a2_r, a3_s, a3_r, a4_s, a4_r, v1_s, v1_r, v2_s, v2_r, v3_s, v3_r, v4_s, v4_r,
):
    ranks, i_dev = nf_ref.shape
    j_dev, k_dev = pf_ref.shape[1], tf_ref.shape[1]
    neurons = i_dev * lax.axis_size("neuron")
    positions = j_dev * lax.axis_size("pos")
    trials = k_dev * lax.axis_size("trial")
    chunks = counts.shape[0]
    k_chunk = k_dev // chunks
    rows = k_chunk * j_dev

    loads = []
    for chunk in range(chunks):
        load = pltpu.make_async_copy(
            counts_hbm.at[pl.ds(chunk * k_chunk, k_chunk)], counts.at[chunk], counts_sem.at[chunk]
        )
        load.start()
        loads.append(load)

    me, y, z_hi = lax.axis_index("neuron"), lax.axis_index("pos"), lax.axis_index("trial")
    core, x, z_lo = lax.rem(me, 2), lax.rem(me // 2, 4), me // 8
    z = z_hi * 4 + z_lo
    sign = 1 - 2 * core
    steps_z = (0, 1, -1, 2 * sign)
    xs = [lax.rem(x + 4 + d, 4) for d in RING]
    xs_back = [lax.rem(x + 4 - d, 4) for d in RING]
    ys = [lax.rem(y + 4 + d, 4) for d in RING]
    ys_back = [lax.rem(y + 4 - d, 4) for d in RING]
    zs = [lax.rem(z + 16 + d, 16) for d in steps_z]
    zs_back = [lax.rem(z + 16 - d, 16) for d in steps_z]
    his = [lax.rem(z_hi + 4 + d, 4) for d in RING]
    his_back = [lax.rem(z_hi + 4 - d, 4) for d in RING]

    def at(x_, y_, z_, core_):
        return {"neuron": (lax.rem(z_, 4) * 4 + x_) * 2 + core_, "pos": y_, "trial": z_ // 4}

    def column(x_, z_):
        return (lax.rem(z_, 4) * 4 + x_) * 2 * i_dev

    cube = [(a, b, c) for c in (3, 1, 2, 0) for b in (3, 1, 2, 0) for a in (3, 1, 2, 0) if a or b or c]

    barrier = pltpu.get_barrier_semaphore()
    greeted = 0
    for a, b, c in cube:
        pl.semaphore_signal(barrier, inc=1, device_id=at(xs_back[a], ys_back[b], zs_back[c], core), device_id_type=MESH)
        greeted += 1
    for a in range(4):
        pl.semaphore_signal(barrier, inc=1, device_id=at(xs_back[a], y, z, 1 - core), device_id_type=MESH)
        greeted += 1
    for h in (1, 2, 3):
        pl.semaphore_signal(barrier, inc=1, device_id={"neuron": me, "pos": y, "trial": his_back[h]}, device_id_type=MESH)
        greeted += 1

    nf, pf, tf = nf_ref[...], pf_ref[...], tf_ref[...]
    stage[...] = jnp.zeros_like(stage)
    for group in range(4):
        stage[pl.ds(group * ranks, ranks), pl.ds(0, j_dev)] = pf
        stage[pl.ds(group * ranks, ranks), pl.ds(j_dev, k_dev)] = tf
    turned = stage[...].T
    pf_t, tf_t = turned[:j_dev], turned[j_dev : j_dev + k_dev]
    lane = lax.broadcasted_iota(jnp.int32, (j_dev, LANES), 1)
    use_high = lax.rem(lane // ranks, 2) == 0
    nf_high, nf_low = split(nf)
    blank = jnp.zeros((LANES - 4 * ranks, i_dev), jnp.float32)
    nf_model = jnp.concatenate([nf_high, nf_high, nf_low, nf_low, blank], axis=0).astype(jnp.bfloat16)
    blank = jnp.zeros((LANES - 2 * ranks, i_dev), jnp.float32)
    nf_proj = jnp.concatenate([nf_high, nf_low, blank], axis=0).astype(jnp.bfloat16)
    pf_pair = jnp.concatenate([pf, pf], axis=1)
    left = lax.broadcasted_iota(jnp.int32, (ranks, LANES), 1) < j_dev

    half = 256
    acc = [jnp.zeros((2 * ranks, half), jnp.float32) for _ in range(i_dev // half)]
    for chunk in range(chunks):
        k0 = chunk * k_chunk
        weights_t = []
        for k in range(k0, k0 + k_chunk):
            high, low = split(pf_t * tf_t[k : k + 1])
            weights_t.append(jnp.where(use_high, high, low))
        weights_t = jnp.concatenate(weights_t, axis=0).astype(jnp.bfloat16)
        highs, lows = [], []
        for k in range(k0, k0 + k_chunk, 2):
            high, low = split(pf_pair * jnp.where(left, tf[:, k : k + 1], tf[:, k + 1 : k + 2]))
            highs.append(high)
            lows.append(low)
        weights = jnp.concatenate(
            [jnp.concatenate(highs, axis=1), jnp.concatenate(lows, axis=1)], axis=0
        ).astype(jnp.bfloat16)
        loads[chunk].wait()
        projected = jnp.zeros((rows, LANES), jnp.float32)
        for part in range(i_dev // half):
            cols = slice(part * half, (part + 1) * half)
            model = jnp.dot(weights_t, nf_model[:, cols], preferred_element_type=jnp.float32)
            guess = pl.reciprocal(model, approx=True)
            inverse = guess * (2.0 - model * guess)
            spikes = counts[chunk, :, :, cols].reshape(rows, half).astype(jnp.float32)
            ratio = 1.0 - spikes * inverse
            high = ratio.astype(jnp.bfloat16)
            low = (ratio - high.astype(jnp.float32)).astype(jnp.bfloat16)
            for piece in (high, low):
                acc[part] = acc[part] + jnp.dot(weights, piece, preferred_element_type=jnp.float32)
                projected = projected + lax.dot_general(
                    piece, nf_proj[:, cols], (((1,), (1,)), ((), ())), preferred_element_type=jnp.float32
                )
        proj[pl.ds(k0 * j_dev, rows), :] = projected
    for part in range(i_dev // half):
        part_a[:, pl.ds(part * half, half)] = (acc[part][:ranks] + acc[part][ranks:]) / (positions * trials)

    pl.semaphore_wait(barrier, greeted)

    def send(src, dst, send_sem, recv_sem, device):
        copy = pltpu.make_async_remote_copy(
            src_ref=src, dst_ref=dst, send_sem=send_sem, recv_sem=recv_sem, device_id=device, device_id_type=MESH
        )
        copy.start()
        return copy

    quarter = i_dev // 4

    def quarter_of(index):
        return part_a.at[:, pl.ds(pl.multiple_of(index * quarter, quarter), quarter)]

    first_a = [
        send(quarter_of(ys[d]), a1.at[d - 1], a1_s.at[d - 1], a1_r.at[d - 1], {"neuron": me, "pos": ys[d], "trial": z_hi})
        for d in (3, 1, 2)
    ]

    grad_b = jnp.zeros((j_dev, LANES), jnp.float32)
    grad_c = []
    for k in range(k_dev):
        block = proj[pl.ds(k * j_dev, j_dev), :]
        grad_b = grad_b + block * tf_t[k : k + 1]
        grad_c.append(jnp.sum(block * pf_t, axis=0, keepdims=True))
    stage[pl.ds(0, j_dev), :] = grad_b / (neurons * trials)
    stage[pl.ds(j_dev, LANES - j_dev), :] = jnp.zeros((LANES - j_dev, LANES), jnp.float32)
    stage[pl.ds(pl.multiple_of(j_dev + z_hi * k_dev, k_dev), k_dev), :] = jnp.concatenate(grad_c, axis=0) / (
        neurons * positions
    )
    turned = stage[...].T
    part_v[...] = (turned[:ranks] + turned[ranks : 2 * ranks]).reshape(part_v.shape)
    first_v = []
    for a in range(4):
        for c in range(2):
            if a or c:
                other_core = core if c == 0 else 1 - core
                slot = a * 2 + c - 1
                first_v.append(
                    send(part_v.at[other_core], v1.at[slot], v1_s.at[slot], v1_r.at[slot], at(xs[a], y, z, other_core))
                )

    for copy in first_a:
        copy.wait_recv()
    sum_a[...] = (a1[0] + a1[1]) + (a1[2] + quarter_of(y)[...])
    second_a = [
        send(sum_a, a2.at[h - 1], a2_s.at[h - 1], a2_r.at[h - 1], {"neuron": me, "pos": y, "trial": his[h]})
        for h in (3, 1, 2)
    ]
    for copy in first_v:
        copy.wait_recv()
    total = part_v[core]
    for slot in range(7):
        total = total + v1[slot]
    sum_v[...] = total
    second_v = [
        send(sum_v, v2.at[h - 1], v2_s.at[h - 1], v2_r.at[h - 1], {"neuron": me, "pos": y, "trial": his[h]})
        for h in (3, 1, 2)
    ]

    for copy in second_a:
        copy.wait_recv()
    mine = gn_ref.at[:, pl.ds(pl.multiple_of(me * i_dev + y * quarter, quarter), quarter)]
    mine[...] = (a2[0] + a2[1]) + (a2[2] + sum_a[...])
    for a, b, c in cube:
        send(mine, mine, a3_s, a3_r.at[c * 4 + a], at(xs[a], ys[b], zs[c], core))
    for copy in second_v:
        copy.wait_recv()
    mean_v[...] = (v2[0] + v2[1]) + (v2[2] + sum_v[...])
    third_v = []
    for b in (3, 1, 2, 0):
        for c in (3, 1, 2, 0):
            if b or c:
                slot = c * 4 + b
                third_v.append(
                    send(mean_v, v3.at[slot], v3_s.at[slot], v3_r.at[slot], at(x, ys[b], zs[c], core))
                )
    v3[0] = mean_v[...]

    partner = {"neuron": me + sign, "pos": y, "trial": z_hi}

    def block_of(start):
        return gn_ref.at[:, pl.ds(pl.multiple_of(start, i_dev), i_dev)]

    fourth = []
    for c in (0, 1, 2, 3):
        for a in (0, 1, 2, 3):
            slot = c * 4 + a
            block = block_of(column(xs_back[a], zs_back[c]) + core * i_dev)
            if slot == 0:
                landed = gn_ref.at[:, pl.ds(0, 3 * quarter)]
            else:
                landed = block
            pltpu.make_async_copy(landed, landed, a3_r.at[slot]).wait()
            fourth.append(send(block, block, a4_s.at[slot], a4_r.at[slot], partner))
    for copy in third_v:
        copy.wait_recv()
    all_c = jnp.zeros((8, LANES), jnp.float32)
    for b in range(4):
        over_z = (v3[b] + v3[4 + b]) + (v3[8 + b] + v3[12 + b])
        all_c = all_c + over_z
        far_v[ys_back[b]] = over_z
    final[4] = all_c
    for b in range(4):
        final[b] = far_v[b]
    swap = send(final, other, v4_s, v4_r, partner)

    def write(ref, row):
        for b in range(4):
            gp_ref[pl.ds(row, 8), pl.ds(b * j_dev, j_dev)] = ref[b][:, :j_dev]
        gt_ref[pl.ds(row, 8), :] = ref[4][:, j_dev:]

    write(final, pl.multiple_of(core * 8, 8))
    swap.wait_recv()
    write(other, pl.multiple_of((1 - core) * 8, 8))
    for copy in fourth:
        copy.wait_recv()

    for copy in first_a + first_v + second_a + second_v + third_v + fourth + [swap]:
        copy.wait_send()
    sent = gn_ref.at[:, pl.ds(0, len(cube) * quarter)]
    pltpu.make_async_copy(sent, sent, a3_s).wait()


def body(counts, neuron_factors, pos_factors, trial_factors):
    k_dev, j_dev, i_dev = counts.shape
    ranks = neuron_factors.shape[0]
    chunks = 4
    vmem = pl.BlockSpec(memory_space=pltpu.VMEM)
    f32 = jnp.float32
    dma = pltpu.SemaphoreType.DMA
    return pl.pallas_call(
        kernel,
        name="gradients",
        out_shape=(
            jax.ShapeDtypeStruct((ranks, i_dev * lax.axis_size("neuron")), f32),
            jax.ShapeDtypeStruct((ranks, j_dev * lax.axis_size("pos")), f32),
            jax.ShapeDtypeStruct((ranks, k_dev * lax.axis_size("trial")), f32),
        ),
        in_specs=[pl.BlockSpec(memory_space=pl.ANY), vmem, vmem, vmem],
        out_specs=(vmem, vmem, vmem),
        scratch_shapes=[
            pltpu.VMEM((chunks, k_dev // chunks, j_dev, i_dev), jnp.int32),
            pltpu.VMEM((LANES, LANES), f32),
            pltpu.VMEM((k_dev * j_dev, LANES), f32),
            pltpu.VMEM((ranks, i_dev), f32),
            pltpu.VMEM((ranks, LANES), f32),
            pltpu.VMEM((2, 8, LANES), f32),
            pltpu.VMEM((8, LANES), f32),
            pltpu.VMEM((8, LANES), f32),
            pltpu.VMEM((4, 8, LANES), f32),
            pltpu.VMEM((5, 8, LANES), f32),
            pltpu.VMEM((3, ranks, LANES), f32),
            pltpu.VMEM((3, ranks, LANES), f32),
            pltpu.VMEM((7, 8, LANES), f32),
            pltpu.VMEM((3, 8, LANES), f32),
            pltpu.VMEM((16, 8, LANES), f32),
            pltpu.VMEM((5, 8, LANES), f32),
            dma((chunks,)),
            dma((3,)), dma((3,)), dma((3,)), dma((3,)),
            dma, dma((16,)), dma((16,)), dma((16,)),
            dma((7,)), dma((7,)), dma((3,)), dma((3,)),
            dma((16,)), dma((16,)), dma, dma,
        ],
        compiler_params=pltpu.CompilerParams(
            collective_id=0, has_side_effects=True, vmem_limit_bytes=32 << 20
        ),
    )(counts, neuron_factors, pos_factors, trial_factors)


def solution(mesh):
    placed = (P("trial", "pos", "neuron"), P(None, "neuron"), P(None, "pos"), P(None, "trial"))
    return jax.shard_map(
        body, mesh=mesh, in_specs=placed, out_specs=(P(), P(), P()), check_vma=False
    )
```

time: 824 us -> 47.2 us (0.06)
  the two profiles are of different devices: /device:TPU:32 before, /device:TPU:1 now
where the time goes in v1:
time: 47.2 us; the launch traced here: 46.9 us
  Pallas kernels  40.3 us (85%)
  local copies, waits for them, and re-layouts  5.91 us (13%)
  between operations  0.65 us (1%)
    pallas_call x1, Pallas kernels, body(): pl.pallas_call(kernel, name='gradients', out_shape=(jax.ShapeDtypeStruct(...  40.3 us
    unnamed x11, local copies, waits for them, and re-layouts  5.91 us

profile of v1, /device:TPU:1, one launch (start us, length us, event | category | flops | bytes accessed | tf_op | source)
XLA Modules:
  0.0 46.9 jit_solution(13169377856126030827)
XLA Ops:
  0.6 0.0 copy-start
  0.6 1.6 %copy-done = s32[16,64,512]{2,1,0:T(8,128)S(1)} copy-done((s32[16,64,512]{2,1,0:T(8,128)S(1)}, s32[16,64,512]{2,1,0:T(8,128)}, u32[]{:S(2)}) %copy-start) | copy-done | bytes 2097176
  2.2 0.0 copy-start.1
  2.2 0.8 %copy-done.1 = f32[16,512]{1,0:T(8,128)S(1)} copy-done((f32[16,512]{1,0:T(8,128)S(1)}, f32[16,512]{1,0:T(8,128)}, u32[]{:S(2)}) %copy-start.1) | copy-done | bytes 32792
  3.0 0.0 copy-start.2
  3.0 0.7 %copy-done.2 = f32[16,64]{1,0:T(8,128)S(1)} copy-done((f32[16,64]{1,0:T(8,128)S(1)}, f32[16,64]{1,0:T(8,128)}, u32[]{:S(2)}) %copy-start.2) | copy-done | bytes 4120
  3.7 0.0 copy-start.3
  3.7 0.7 %copy-done.3 = f32[16,16]{1,0:T(8,128)S(1)} copy-done((f32[16,16]{1,0:T(8,128)S(1)}, f32[16,16]{1,0:T(8,128)}, u32[]{:S(2)}) %copy-start.3) | copy-done | bytes 1048
  4.4 40.3 %gradients.1 = (f32[16,16384]{1,0:T(8,128)S(1)}, f32[16,256]{1,0:T(8,128)S(1)}, f32[16,64]{1,0:T(8,128)S(1)}) custom-call(s32[16,64,512]{2,1,0:T(8,128)S(1)} %copy-done, f32[16,512]{1,0:T(8,128)S(1)} %copy-done.1, f32[16,64]{1,0:T(8,128)S(1)} %copy-done.2, f32[16,16]{1,0:T(8,128)S(1)} %copy-done.3), custom_call_target="tpu_custom_call" | custom-call | tf_op jit(solution)/shard_map/gradients/pallas_call | solution.py:260
  44.7 1.0 %copy.10 = f32[16,16384]{1,0:T(8,128)} copy(f32[16,16384]{1,0:T(8,128)S(1)} %get-tuple-element.6) | data formatting | bytes 2097152
  45.7 0.6 %copy.11 = f32[16,256]{1,0:T(8,128)} copy(f32[16,256]{1,0:T(8,128)S(1)} %get-tuple-element.7) | data formatting | bytes 32768
  46.3 0.6 %copy.12 = f32[16,64]{1,0:T(8,128)} copy(f32[16,64]{1,0:T(8,128)S(1)} %get-tuple-element.8) | data formatting | bytes 8192
Async XLA Ops:
  0.6 1.6 %copy-start = (s32[16,64,512]{2,1,0:T(8,128)S(1)}, s32[16,64,512]{2,1,0:T(8,128)}, u32[]{:S(2)}) copy-start(s32[16,64,512]{2,1,0:T(8,128)} %counts_hbm.1) | copy-start | bytes 6291460
  2.2 0.8 %copy-start.1 = (f32[16,512]{1,0:T(8,128)S(1)}, f32[16,512]{1,0:T(8,128)}, u32[]{:S(2)}) copy-start(f32[16,512]{1,0:T(8,128)} %nf_ref.1) | copy-start | bytes 98308
  3.0 0.7 %copy-start.2 = (f32[16,64]{1,0:T(8,128)S(1)}, f32[16,64]{1,0:T(8,128)}, u32[]{:S(2)}) copy-start(f32[16,64]{1,0:T(8,128)} %pf_ref.1) | copy-start | bytes 12292
  3.7 0.7 %copy-start.3 = (f32[16,16]{1,0:T(8,128)S(1)}, f32[16,16]{1,0:T(8,128)}, u32[]{:S(2)}) copy-start(f32[16,16]{1,0:T(8,128)} %tf_ref.1) | copy-start | bytes 3076

commit v2 on v1

--- a/solution.py
+++ b/solution.py
@@ -8,6 +8,13 @@
 MESH = pl.DeviceIdType.MESH
 RING = (0, 1, -1, 2)
 LANES = 128
+ORDER_X = (3, 1, 2, 0)
+ORDER_Y = (3, 1, 2, 0)
+ORDER_Z = (3, 1, 2, 0)
+EARLY = 24
+HALF = 256
+CHUNKS = 1
+STORES = 4
 
 
 def split(value):
@@ -16,10 +23,11 @@
 
 
 def kernel(
-    counts_hbm, nf_ref, pf_ref, tf_ref, gn_ref, gp_ref, gt_ref,
-    counts, stage, proj, part_a, sum_a, part_v, sum_v, mean_v, far_v, final,
+    counts_hbm, nf_hbm, pf_hbm, tf_hbm, gn_ref, gp_ref, gt_ref,
+    nf_ref, pf_ref, tf_ref, counts, stage, proj, part_a, sum_a, part_v, sum_v, mean_v, far_v, final,
     a1, a2, v1, v2, v3, other,
-    counts_sem, a1_s, a1_r, a2_s, a2_r, a3_s, a3_r, a4_s, a4_r, v1_s, v1_r, v2_s, v2_r, v3_s, v3_r, v4_s, v4_r,
+    factor_sem, counts_sem, a1_s, a1_r, a2_s, a2_r, a3_s, a3_r, a4_s, a4_r, v1_s, v1_r, v2_s, v2_r, v3_s, v3_r, v4_s, v4_r,
+    plane_sem, cube_sem,
 ):
     ranks, i_dev = nf_ref.shape
     j_dev, k_dev = pf_ref.shape[1], tf_ref.shape[1]
@@ -30,6 +38,11 @@
     k_chunk = k_dev // chunks
     rows = k_chunk * j_dev
 
+    factors = []
+    for at_sem, (src, dst) in enumerate(((pf_hbm, pf_ref), (tf_hbm, tf_ref), (nf_hbm, nf_ref))):
+        load = pltpu.make_async_copy(src, dst, factor_sem.at[at_sem])
+        load.start()
+        factors.append(load)
     loads = []
     for chunk in range(chunks):
         load = pltpu.make_async_copy(
@@ -58,20 +71,20 @@
     def column(x_, z_):
         return (lax.rem(z_, 4) * 4 + x_) * 2 * i_dev
 
-    cube = [(a, b, c) for c in (3, 1, 2, 0) for b in (3, 1, 2, 0) for a in (3, 1, 2, 0) if a or b or c]
+    cube = [(a, b, c) for c in ORDER_Z for b in ORDER_Y for a in ORDER_X if a or b or c]
 
     barrier = pltpu.get_barrier_semaphore()
-    greeted = 0
-    for a, b, c in cube:
-        pl.semaphore_signal(barrier, inc=1, device_id=at(xs_back[a], ys_back[b], zs_back[c], core), device_id_type=MESH)
-        greeted += 1
-    for a in range(4):
-        pl.semaphore_signal(barrier, inc=1, device_id=at(xs_back[a], y, z, 1 - core), device_id_type=MESH)
-        greeted += 1
-    for h in (1, 2, 3):
-        pl.semaphore_signal(barrier, inc=1, device_id={"neuron": me, "pos": y, "trial": his_back[h]}, device_id_type=MESH)
-        greeted += 1
-
+    greeted = [at(xs_back[a], y, z, core) for a in (1, 2, 3)]
+    greeted += [at(xs_back[a], y, z, 1 - core) for a in range(4)]
+    greeted += [at(x, ys_back[b], z, core) for b in (1, 2, 3)]
+    greeted += [at(x, y, zs_back[c], core) for c in (1, 2, 3)]
+    greeted += [at(x, y, zs[3], core)]
+    greeted += [{"neuron": me, "pos": y, "trial": his_back[h]} for h in (1, 2, 3)]
+    for device in greeted:
+        pl.semaphore_signal(barrier, inc=1, device_id=device, device_id_type=MESH)
+
+    for load in factors:
+        load.wait()
     nf, pf, tf = nf_ref[...], pf_ref[...], tf_ref[...]
     stage[...] = jnp.zeros_like(stage)
     for group in range(4):
@@ -85,32 +98,32 @@
     blank = jnp.zeros((LANES - 4 * ranks, i_dev), jnp.float32)
     nf_model = jnp.concatenate([nf_high, nf_high, nf_low, nf_low, blank], axis=0).astype(jnp.bfloat16)
     blank = jnp.zeros((LANES - 2 * ranks, i_dev), jnp.float32)
-    nf_proj = jnp.concatenate([nf_high, nf_low, blank], axis=0).astype(jnp.bfloat16)
+    nf_proj = jnp.concatenate([nf_high, nf_low, blank], axis=0).T.astype(jnp.bfloat16)
     pf_pair = jnp.concatenate([pf, pf], axis=1)
     left = lax.broadcasted_iota(jnp.int32, (ranks, LANES), 1) < j_dev
 
-    half = 256
+    half = HALF
     acc = [jnp.zeros((2 * ranks, half), jnp.float32) for _ in range(i_dev // half)]
+    weights_t, weights = [], []
+    for k in range(k_dev):
+        high, low = split(pf_t * tf_t[k : k + 1])
+        weights_t.append(jnp.where(use_high, high, low).astype(jnp.bfloat16))
+    for k in range(0, k_dev, 2):
+        high, low = split(pf_pair * jnp.where(left, tf[:, k : k + 1], tf[:, k + 1 : k + 2]))
+        weights.append(jnp.concatenate([high, low], axis=0).astype(jnp.bfloat16))
     for chunk in range(chunks):
         k0 = chunk * k_chunk
-        weights_t = []
-        for k in range(k0, k0 + k_chunk):
-            high, low = split(pf_t * tf_t[k : k + 1])
-            weights_t.append(jnp.where(use_high, high, low))
-        weights_t = jnp.concatenate(weights_t, axis=0).astype(jnp.bfloat16)
-        highs, lows = [], []
-        for k in range(k0, k0 + k_chunk, 2):
-            high, low = split(pf_pair * jnp.where(left, tf[:, k : k + 1], tf[:, k + 1 : k + 2]))
-            highs.append(high)
-            lows.append(low)
-        weights = jnp.concatenate(
-            [jnp.concatenate(highs, axis=1), jnp.concatenate(lows, axis=1)], axis=0
-        ).astype(jnp.bfloat16)
+        chunk_t = jnp.concatenate(weights_t[k0 : k0 + k_chunk], axis=0)
+        chunk_w = jnp.concatenate(weights[k0 // 2 : (k0 + k_chunk) // 2], axis=1)
+        models = [
+            jnp.dot(chunk_t, nf_model[:, part * half : (part + 1) * half], preferred_element_type=jnp.float32)
+            for part in range(i_dev // half)
+        ]
         loads[chunk].wait()
         projected = jnp.zeros((rows, LANES), jnp.float32)
         for part in range(i_dev // half):
             cols = slice(part * half, (part + 1) * half)
-            model = jnp.dot(weights_t, nf_model[:, cols], preferred_element_type=jnp.float32)
+            model = models[part]
             guess = pl.reciprocal(model, approx=True)
             inverse = guess * (2.0 - model * guess)
             spikes = counts[chunk, :, :, cols].reshape(rows, half).astype(jnp.float32)
@@ -118,15 +131,15 @@
             high = ratio.astype(jnp.bfloat16)
             low = (ratio - high.astype(jnp.float32)).astype(jnp.bfloat16)
             for piece in (high, low):
-                acc[part] = acc[part] + jnp.dot(weights, piece, preferred_element_type=jnp.float32)
-                projected = projected + lax.dot_general(
-                    piece, nf_proj[:, cols], (((1,), (1,)), ((), ())), preferred_element_type=jnp.float32
-                )
+                acc[part] = acc[part] + jnp.dot(chunk_w, piece, preferred_element_type=jnp.float32)
+                projected = projected + jnp.dot(piece, nf_proj[cols], preferred_element_type=jnp.float32)
         proj[pl.ds(k0 * j_dev, rows), :] = projected
     for part in range(i_dev // half):
         part_a[:, pl.ds(part * half, half)] = (acc[part][:ranks] + acc[part][ranks:]) / (positions * trials)
 
-    pl.semaphore_wait(barrier, greeted)
+    pl.semaphore_wait(barrier, len(greeted))
+    for a in (1, 2, 3):
+        pl.semaphore_signal(plane_sem, inc=1, device_id=at(xs_back[a], y, z, core), device_id_type=MESH)
 
     def send(src, dst, send_sem, recv_sem, device):
         copy = pltpu.make_async_remote_copy(
@@ -135,13 +148,14 @@
         copy.start()
         return copy
 
-    quarter = i_dev // 4
-
-    def quarter_of(index):
-        return part_a.at[:, pl.ds(pl.multiple_of(index * quarter, quarter), quarter)]
+    tall, wide = ranks // 2, i_dev // 2
+
+    def quarter_of(ref, index, start):
+        row, col = (index // 2) * tall, start + lax.rem(index, 2) * wide
+        return ref.at[pl.ds(pl.multiple_of(row, tall), tall), pl.ds(pl.multiple_of(col, wide), wide)]
 
     first_a = [
-        send(quarter_of(ys[d]), a1.at[d - 1], a1_s.at[d - 1], a1_r.at[d - 1], {"neuron": me, "pos": ys[d], "trial": z_hi})
+        send(quarter_of(part_a, ys[d], 0), a1.at[d - 1], a1_s.at[d - 1], a1_r.at[d - 1], {"neuron": me, "pos": ys[d], "trial": z_hi})
         for d in (3, 1, 2)
     ]
 
@@ -170,11 +184,14 @@
 
     for copy in first_a:
         copy.wait_recv()
-    sum_a[...] = (a1[0] + a1[1]) + (a1[2] + quarter_of(y)[...])
+    sum_a[...] = (a1[0] + a1[1]) + (a1[2] + quarter_of(part_a, y, 0)[...])
     second_a = [
         send(sum_a, a2.at[h - 1], a2_s.at[h - 1], a2_r.at[h - 1], {"neuron": me, "pos": y, "trial": his[h]})
         for h in (3, 1, 2)
     ]
+    pl.semaphore_wait(plane_sem, 3)
+    for c in (1, 2, 3):
+        pl.semaphore_signal(cube_sem, inc=1, device_id=at(x, y, zs_back[c], core), device_id_type=MESH)
     for copy in first_v:
         copy.wait_recv()
     total = part_v[core]
@@ -188,21 +205,27 @@
 
     for copy in second_a:
         copy.wait_recv()
-    mine = gn_ref.at[:, pl.ds(pl.multiple_of(me * i_dev + y * quarter, quarter), quarter)]
+    mine = quarter_of(gn_ref, y, me * i_dev)
     mine[...] = (a2[0] + a2[1]) + (a2[2] + sum_a[...])
-    for a, b, c in cube:
-        send(mine, mine, a3_s, a3_r.at[c * 4 + a], at(xs[a], ys[b], zs[c], core))
+    pl.semaphore_wait(cube_sem, 3)
+
+    def spread(steps):
+        for a, b, c in steps:
+            send(mine, mine, a3_s, a3_r.at[c * 4 + a], at(xs[a], ys[b], zs[c], core))
+
+    spread(cube[:EARLY])
     for copy in second_v:
         copy.wait_recv()
     mean_v[...] = (v2[0] + v2[1]) + (v2[2] + sum_v[...])
     third_v = []
-    for b in (3, 1, 2, 0):
-        for c in (3, 1, 2, 0):
+    for b in ORDER_Y:
+        for c in ORDER_Z:
             if b or c:
                 slot = c * 4 + b
                 third_v.append(
                     send(mean_v, v3.at[slot], v3_s.at[slot], v3_r.at[slot], at(x, ys[b], zs[c], core))
                 )
+    spread(cube[EARLY:])
     v3[0] = mean_v[...]
 
     partner = {"neuron": me + sign, "pos": y, "trial": z_hi}
@@ -211,12 +234,12 @@
         return gn_ref.at[:, pl.ds(pl.multiple_of(start, i_dev), i_dev)]
 
     fourth = []
-    for c in (0, 1, 2, 3):
-        for a in (0, 1, 2, 3):
+    for c in ORDER_Z:
+        for a in ORDER_X:
             slot = c * 4 + a
             block = block_of(column(xs_back[a], zs_back[c]) + core * i_dev)
             if slot == 0:
-                landed = gn_ref.at[:, pl.ds(0, 3 * quarter)]
+                landed = gn_ref.at[pl.ds(0, tall), pl.ds(0, 3 * wide)]
             else:
                 landed = block
             pltpu.make_async_copy(landed, landed, a3_r.at[slot]).wait()
@@ -246,54 +269,80 @@
 
     for copy in first_a + first_v + second_a + second_v + third_v + fourth + [swap]:
         copy.wait_send()
-    sent = gn_ref.at[:, pl.ds(0, len(cube) * quarter)]
+    sent = gn_ref.at[pl.ds(0, tall), pl.ds(0, len(cube) * wide)]
     pltpu.make_async_copy(sent, sent, a3_s).wait()
+
+
+def store(gn_ref, gp_ref, gt_ref, gn_hbm, gp_hbm, gt_hbm, sem):
+    width = gn_ref.shape[1] // STORES
+    copies = [
+        pltpu.make_async_copy(gn_ref.at[:, pl.ds(i * width, width)], gn_hbm.at[:, pl.ds(i * width, width)], sem.at[i])
+        for i in range(STORES)
+    ]
+    copies.append(pltpu.make_async_copy(gp_ref, gp_hbm, sem.at[STORES]))
+    copies.append(pltpu.make_async_copy(gt_ref, gt_hbm, sem.at[STORES + 1]))
+    for copy in copies:
+        copy.start()
+    for copy in copies:
+        copy.wait()
 
 
 def body(counts, neuron_factors, pos_factors, trial_factors):
     k_dev, j_dev, i_dev = counts.shape
     ranks = neuron_factors.shape[0]
-    chunks = 4
+    chunks = CHUNKS
     vmem = pl.BlockSpec(memory_space=pltpu.VMEM)
     f32 = jnp.float32
     dma = pltpu.SemaphoreType.DMA
-    return pl.pallas_call(
+    gathered = pl.pallas_call(
         kernel,
         name="gradients",
         out_shape=(
-            jax.ShapeDtypeStruct((ranks, i_dev * lax.axis_size("neuron")), f32),
-            jax.ShapeDtypeStruct((ranks, j_dev * lax.axis_size("pos")), f32),
-            jax.ShapeDtypeStruct((ranks, k_dev * lax.axis_size("trial")), f32),
+            pltpu.VMEM((ranks, i_dev * lax.axis_size("neuron")), f32),
+            pltpu.VMEM((ranks, j_dev * lax.axis_size("pos")), f32),
+            pltpu.VMEM((ranks, k_dev * lax.axis_size("trial")), f32),
         ),
-        in_specs=[pl.BlockSpec(memory_space=pl.ANY), vmem, vmem, vmem],
+        in_specs=[pl.BlockSpec(memory_space=pltpu.HBM)] * 4,
         out_specs=(vmem, vmem, vmem),
         scratch_shapes=[
+            pltpu.VMEM((ranks, i_dev), f32),
+            pltpu.VMEM((ranks, j_dev), f32),
+            pltpu.VMEM((ranks, k_dev), f32),
             pltpu.VMEM((chunks, k_dev // chunks, j_dev, i_dev), jnp.int32),
             pltpu.VMEM((LANES, LANES), f32),
             pltpu.VMEM((k_dev * j_dev, LANES), f32),
             pltpu.VMEM((ranks, i_dev), f32),
-            pltpu.VMEM((ranks, LANES), f32),
+            pltpu.VMEM((ranks // 2, i_dev // 2), f32),
             pltpu.VMEM((2, 8, LANES), f32),
             pltpu.VMEM((8, LANES), f32),
             pltpu.VMEM((8, LANES), f32),
             pltpu.VMEM((4, 8, LANES), f32),
             pltpu.VMEM((5, 8, LANES), f32),
-            pltpu.VMEM((3, ranks, LANES), f32),
-            pltpu.VMEM((3, ranks, LANES), f32),
+            pltpu.VMEM((3, ranks // 2, i_dev // 2), f32),
+            pltpu.VMEM((3, ranks // 2, i_dev // 2), f32),
             pltpu.VMEM((7, 8, LANES), f32),
             pltpu.VMEM((3, 8, LANES), f32),
             pltpu.VMEM((16, 8, LANES), f32),
             pltpu.VMEM((5, 8, LANES), f32),
-            dma((chunks,)),
+            dma((3,)), dma((chunks,)),
             dma((3,)), dma((3,)), dma((3,)), dma((3,)),
             dma, dma((16,)), dma((16,)), dma((16,)),
             dma((7,)), dma((7,)), dma((3,)), dma((3,)),
             dma((16,)), dma((16,)), dma, dma,
+            pltpu.SemaphoreType.REGULAR, pltpu.SemaphoreType.REGULAR,
         ],
         compiler_params=pltpu.CompilerParams(
             collective_id=0, has_side_effects=True, vmem_limit_bytes=32 << 20
         ),
-    )(counts, neuron_factors, pos_factors, trial_factors)
+    )(*(pltpu.with_memory_space_constraint(one, pltpu.HBM) for one in (counts, neuron_factors, pos_factors, trial_factors)))
+    return pl.pallas_call(
+        store,
+        name="store",
+        out_shape=tuple(jax.ShapeDtypeStruct(one.shape, f32) for one in gathered),
+        in_specs=[vmem] * 3,
+        out_specs=(pl.BlockSpec(memory_space=pltpu.HBM),) * 3,
+        scratch_shapes=[dma((STORES + 2,))],
+    )(*(pltpu.with_memory_space_constraint(one, pltpu.VMEM) for one in gathered))
 
 
 def solution(mesh):

time: 47.2 us -> 42 us (0.89)
  local copies, waits for them, and re-layouts: 5.91 us -> 0 us
  Pallas kernels: 40.3 us -> 41.2 us
    unnamed x11 -> x0, local copies, waits for them, and re-layouts: 5.91 us -> none
    pallas_call x1 -> x2, Pallas kernels: 40.3 us -> 41.2 us  [the longest x1 40.2 us: body(): pl.pallas_call(kernel, name='gradients', out_shape=(pltpu.VMEM((ranks, i_...]
where the time goes in v2:
time: 42 us; the launch traced here: 41.9 us
  Pallas kernels  41.2 us (98%)
  between operations  0.64 us (2%)
    pallas_call x1, Pallas kernels, body(): pl.pallas_call(kernel, name='gradients', out_shape=(pltpu.VMEM((ranks, i_...  40.2 us
    pallas_call x1, Pallas kernels, body(): pl.pallas_call(store, name='store', out_shape=tuple((jax.ShapeDtypeStruct...  1.02 us

profile of v2, /device:TPU:1, one launch (start us, length us, event | category | flops | bytes accessed | tf_op | source)
XLA Modules:
  0.0 41.9 jit_solution(17389579579990809320)
XLA Ops:
  0.6 40.2 %gradients.1 = (f32[16,16384]{1,0:T(8,128)S(1)}, f32[16,256]{1,0:T(8,128)S(1)}, f32[16,64]{1,0:T(8,128)S(1)}) custom-call(s32[16,64,512]{2,1,0:T(8,128)} %counts_hbm.1, f32[16,512]{1,0:T(8,128)} %nf_hbm.1, f32[16,64]{1,0:T(8,128)} %pf_hbm.1, f32[16,16]{1,0:T(8,128)} %tf_hbm.1), custom_call_target="tpu_custom_call" | custom-call | tf_op jit(solution)/shard_map/gradients/pallas_call | solution.py:297
  40.9 1.0 %store.1 = (f32[16,16384]{1,0:T(8,128)}, f32[16,256]{1,0:T(8,128)}, f32[16,64]{1,0:T(8,128)}) custom-call(f32[16,16384]{1,0:T(8,128)S(1)} %get-tuple-element.6.gn_ref, f32[16,256]{1,0:T(8,128)S(1)} %get-tuple-element.7.gp_ref, f32[16,64]{1,0:T(8,128)S(1)} %get-tuple-element.8.gt_ref), custom_call_target="tpu_custom_call" | custom-call | tf_op jit(solution)/shard_map/store/pallas_call | solution.py:338

commit v3 on v2

--- a/solution.py
+++ b/solution.py
@@ -10,8 +10,10 @@
 LANES = 128
 ORDER_X = (3, 1, 2, 0)
 ORDER_Y = (3, 1, 2, 0)
-ORDER_Z = (3, 1, 2, 0)
-EARLY = 24
+ORDER_Z = (0, 1, 3, 2)
+VTURN = 3
+VFIN = 15
+LOADS = 8
 HALF = 256
 CHUNKS = 1
 STORES = 4
@@ -24,7 +26,7 @@
 
 def kernel(
     counts_hbm, nf_hbm, pf_hbm, tf_hbm, gn_ref, gp_ref, gt_ref,
-    nf_ref, pf_ref, tf_ref, counts, stage, proj, part_a, sum_a, part_v, sum_v, mean_v, far_v, final,
+    nf_ref, pf_ref, tf_ref, counts, stage, proj, part_a, sum_a, part_v, sum_v, mean_v, final,
     a1, a2, v1, v2, v3, other,
     factor_sem, counts_sem, a1_s, a1_r, a2_s, a2_r, a3_s, a3_r, a4_s, a4_r, v1_s, v1_r, v2_s, v2_r, v3_s, v3_r, v4_s, v4_r,
     plane_sem, cube_sem,
@@ -34,7 +36,7 @@
     neurons = i_dev * lax.axis_size("neuron")
     positions = j_dev * lax.axis_size("pos")
     trials = k_dev * lax.axis_size("trial")
-    chunks = counts.shape[0]
+    chunks = CHUNKS
     k_chunk = k_dev // chunks
     rows = k_chunk * j_dev
 
@@ -44,9 +46,10 @@
         load.start()
         factors.append(load)
     loads = []
-    for chunk in range(chunks):
+    step = k_dev // LOADS
+    for part in range(LOADS):
         load = pltpu.make_async_copy(
-            counts_hbm.at[pl.ds(chunk * k_chunk, k_chunk)], counts.at[chunk], counts_sem.at[chunk]
+            counts_hbm.at[pl.ds(part * step, step)], counts.at[pl.ds(part * step, step)], counts_sem.at[part]
         )
         load.start()
         loads.append(load)
@@ -55,7 +58,7 @@
     core, x, z_lo = lax.rem(me, 2), lax.rem(me // 2, 4), me // 8
     z = z_hi * 4 + z_lo
     sign = 1 - 2 * core
-    steps_z = (0, 1, -1, 2 * sign)
+    steps_z = (0, 1, 2 * sign, -1)
     xs = [lax.rem(x + 4 + d, 4) for d in RING]
     xs_back = [lax.rem(x + 4 - d, 4) for d in RING]
     ys = [lax.rem(y + 4 + d, 4) for d in RING]
@@ -71,14 +74,12 @@
     def column(x_, z_):
         return (lax.rem(z_, 4) * 4 + x_) * 2 * i_dev
 
-    cube = [(a, b, c) for c in ORDER_Z for b in ORDER_Y for a in ORDER_X if a or b or c]
-
     barrier = pltpu.get_barrier_semaphore()
     greeted = [at(xs_back[a], y, z, core) for a in (1, 2, 3)]
     greeted += [at(xs_back[a], y, z, 1 - core) for a in range(4)]
     greeted += [at(x, ys_back[b], z, core) for b in (1, 2, 3)]
     greeted += [at(x, y, zs_back[c], core) for c in (1, 2, 3)]
-    greeted += [at(x, y, zs[3], core)]
+    greeted += [at(x, y, zs[2], core)]
     greeted += [{"neuron": me, "pos": y, "trial": his_back[h]} for h in (1, 2, 3)]
     for device in greeted:
         pl.semaphore_signal(barrier, inc=1, device_id=device, device_id_type=MESH)
@@ -119,14 +120,15 @@
             jnp.dot(chunk_t, nf_model[:, part * half : (part + 1) * half], preferred_element_type=jnp.float32)
             for part in range(i_dev // half)
         ]
-        loads[chunk].wait()
+        for load in loads[chunk * LOADS // chunks : (chunk + 1) * LOADS // chunks]:
+            load.wait()
         projected = jnp.zeros((rows, LANES), jnp.float32)
         for part in range(i_dev // half):
             cols = slice(part * half, (part + 1) * half)
             model = models[part]
             guess = pl.reciprocal(model, approx=True)
             inverse = guess * (2.0 - model * guess)
-            spikes = counts[chunk, :, :, cols].reshape(rows, half).astype(jnp.float32)
+            spikes = counts[k0 : k0 + k_chunk, :, cols].reshape(rows, half).astype(jnp.float32)
             ratio = 1.0 - spikes * inverse
             high = ratio.astype(jnp.bfloat16)
             low = (ratio - high.astype(jnp.float32)).astype(jnp.bfloat16)
@@ -209,68 +211,82 @@
     mine[...] = (a2[0] + a2[1]) + (a2[2] + sum_a[...])
     pl.semaphore_wait(cube_sem, 3)
 
-    def spread(steps):
-        for a, b, c in steps:
-            send(mine, mine, a3_s, a3_r.at[c * 4 + a], at(xs[a], ys[b], zs[c], core))
-
-    spread(cube[:EARLY])
-    for copy in second_v:
-        copy.wait_recv()
-    mean_v[...] = (v2[0] + v2[1]) + (v2[2] + sum_v[...])
-    third_v = []
-    for b in ORDER_Y:
-        for c in ORDER_Z:
-            if b or c:
-                slot = c * 4 + b
-                third_v.append(
-                    send(mean_v, v3.at[slot], v3_s.at[slot], v3_r.at[slot], at(x, ys[b], zs[c], core))
-                )
-    spread(cube[EARLY:])
-    v3[0] = mean_v[...]
+    below = -1 - core
+    lowest = lax.rem(z + below + 16, 16)
+    first = jnp.where(lowest > 12, 16 - lowest, 0)
+    for turn in range(4):
+        dz = lax.rem(first + turn, 4) + below
+        z_to, c = lax.rem(z + dz + 16, 16), lax.rem(dz + 4, 4)
+        for a in ORDER_X:
+            for b in ORDER_Y:
+
+                def give(a=a, b=b, c=c, z_to=z_to):
+                    send(mine, mine, a3_s, a3_r.at[c * 4 + a], at(xs[a], ys[b], z_to, core))
+
+                if a or b:
+                    give()
+                else:
+                    pl.when(dz != 0)(give)
+        if turn == VTURN:
+            for copy in second_v:
+                copy.wait_recv()
+            mean_v[...] = (v2[0] + v2[1]) + (v2[2] + sum_v[...])
+            v3[0] = mean_v[...]
+        for late in range(turn + 1) if turn == VTURN else (turn,) if turn > VTURN else ():
+            dz = lax.rem(first + late, 4) + below
+            z_to, c = lax.rem(z + dz + 16, 16), lax.rem(dz + 4, 4)
+            for b in ORDER_Y:
+
+                def give_v(b=b, c=c, z_to=z_to):
+                    slot = c * 4 + b
+                    send(mean_v, v3.at[slot], v3_s, v3_r.at[slot], at(x, ys[b], z_to, core))
+
+                if b:
+                    give_v()
+                else:
+                    pl.when(dz != 0)(give_v)
 
     partner = {"neuron": me + sign, "pos": y, "trial": z_hi}
 
     def block_of(start):
         return gn_ref.at[:, pl.ds(pl.multiple_of(start, i_dev), i_dev)]
-
-    fourth = []
-    for c in ORDER_Z:
-        for a in ORDER_X:
-            slot = c * 4 + a
-            block = block_of(column(xs_back[a], zs_back[c]) + core * i_dev)
-            if slot == 0:
-                landed = gn_ref.at[pl.ds(0, tall), pl.ds(0, 3 * wide)]
-            else:
-                landed = block
-            pltpu.make_async_copy(landed, landed, a3_r.at[slot]).wait()
-            fourth.append(send(block, block, a4_s.at[slot], a4_r.at[slot], partner))
-    for copy in third_v:
-        copy.wait_recv()
-    all_c = jnp.zeros((8, LANES), jnp.float32)
-    for b in range(4):
-        over_z = (v3[b] + v3[4 + b]) + (v3[8 + b] + v3[12 + b])
-        all_c = all_c + over_z
-        far_v[ys_back[b]] = over_z
-    final[4] = all_c
-    for b in range(4):
-        final[b] = far_v[b]
-    swap = send(final, other, v4_s, v4_r, partner)
 
     def write(ref, row):
         for b in range(4):
             gp_ref[pl.ds(row, 8), pl.ds(b * j_dev, j_dev)] = ref[b][:, :j_dev]
         gt_ref[pl.ds(row, 8), :] = ref[4][:, j_dev:]
 
-    write(final, pl.multiple_of(core * 8, 8))
+    fourth = []
+    for turn, (a, c) in enumerate((a, c) for a in ORDER_X for c in ORDER_Z):
+        if turn == VFIN:
+            for slot in range(1, 16):
+                pltpu.make_async_copy(v3.at[slot], v3.at[slot], v3_r.at[slot]).wait()
+            all_c = jnp.zeros((8, LANES), jnp.float32)
+            for b in range(4):
+                over_z = (v3[b] + v3[4 + b]) + (v3[8 + b] + v3[12 + b])
+                all_c = all_c + over_z
+                final[ys_back[b]] = over_z
+            final[4] = all_c
+            swap = send(final, other, v4_s, v4_r, partner)
+            write(final, pl.multiple_of(core * 8, 8))
+        slot = c * 4 + a
+        block = block_of(column(xs_back[a], zs_back[c]) + core * i_dev)
+        if slot == 0:
+            landed = gn_ref.at[pl.ds(0, tall), pl.ds(0, 3 * wide)]
+        else:
+            landed = block
+        pltpu.make_async_copy(landed, landed, a3_r.at[slot]).wait()
+        fourth.append(send(block, block, a4_s.at[slot], a4_r.at[slot], partner))
     swap.wait_recv()
     write(other, pl.multiple_of((1 - core) * 8, 8))
     for copy in fourth:
         copy.wait_recv()
 
-    for copy in first_a + first_v + second_a + second_v + third_v + fourth + [swap]:
+    for copy in first_a + first_v + second_a + second_v + fourth + [swap]:
         copy.wait_send()
-    sent = gn_ref.at[pl.ds(0, tall), pl.ds(0, len(cube) * wide)]
+    sent = gn_ref.at[pl.ds(0, tall), pl.ds(0, 63 * wide)]
     pltpu.make_async_copy(sent, sent, a3_s).wait()
+    pltpu.make_async_copy(v3.at[pl.ds(0, 15)], v3.at[pl.ds(0, 15)], v3_s).wait()
 
 
 def store(gn_ref, gp_ref, gt_ref, gn_hbm, gp_hbm, gt_hbm, sem):
@@ -290,7 +306,6 @@
 def body(counts, neuron_factors, pos_factors, trial_factors):
     k_dev, j_dev, i_dev = counts.shape
     ranks = neuron_factors.shape[0]
-    chunks = CHUNKS
     vmem = pl.BlockSpec(memory_space=pltpu.VMEM)
     f32 = jnp.float32
     dma = pltpu.SemaphoreType.DMA
@@ -308,7 +323,7 @@
             pltpu.VMEM((ranks, i_dev), f32),
             pltpu.VMEM((ranks, j_dev), f32),
             pltpu.VMEM((ranks, k_dev), f32),
-            pltpu.VMEM((chunks, k_dev // chunks, j_dev, i_dev), jnp.int32),
+            pltpu.VMEM((k_dev, j_dev, i_dev), jnp.int32),
             pltpu.VMEM((LANES, LANES), f32),
             pltpu.VMEM((k_dev * j_dev, LANES), f32),
             pltpu.VMEM((ranks, i_dev), f32),
@@ -316,7 +331,6 @@
             pltpu.VMEM((2, 8, LANES), f32),
             pltpu.VMEM((8, LANES), f32),
             pltpu.VMEM((8, LANES), f32),
-            pltpu.VMEM((4, 8, LANES), f32),
             pltpu.VMEM((5, 8, LANES), f32),
             pltpu.VMEM((3, ranks // 2, i_dev // 2), f32),
             pltpu.VMEM((3, ranks // 2, i_dev // 2), f32),
@@ -324,11 +338,11 @@
             pltpu.VMEM((3, 8, LANES), f32),
             pltpu.VMEM((16, 8, LANES), f32),
             pltpu.VMEM((5, 8, LANES), f32),
-            dma((3,)), dma((chunks,)),
+            dma((3,)), dma((LOADS,)),
             dma((3,)), dma((3,)), dma((3,)), dma((3,)),
             dma, dma((16,)), dma((16,)), dma((16,)),
             dma((7,)), dma((7,)), dma((3,)), dma((3,)),
-            dma((16,)), dma((16,)), dma, dma,
+            dma, dma((16,)), dma, dma,
             pltpu.SemaphoreType.REGULAR, pltpu.SemaphoreType.REGULAR,
         ],
         compiler_params=pltpu.CompilerParams(

time: 42 us -> 39.9 us (0.950)
  Pallas kernels: 41.2 us -> 39.1 us
    pallas_call x1, Pallas kernels: 40.2 us -> 38.1 us  [body(): pl.pallas_call(kernel, name='gradients', out_shape=(pltpu.VMEM((ranks, i_...]
where the time goes in v3:
time: 39.9 us; the launch traced here: 39.7 us
  Pallas kernels  39.1 us (98%)
  between operations  0.64 us (2%)
    pallas_call x1, Pallas kernels, body(): pl.pallas_call(kernel, name='gradients', out_shape=(pltpu.VMEM((ranks, i_...  38.1 us
    pallas_call x1, Pallas kernels, body(): pl.pallas_call(store, name='store', out_shape=tuple((jax.ShapeDtypeStruct...  1.02 us

profile of v3, /device:TPU:1, one launch (start us, length us, event | category | flops | bytes accessed | tf_op | source)
XLA Modules:
  0.0 39.7 jit_solution(16501858778452076514)
XLA Ops:
  0.6 38.1 %gradients.1 = (f32[16,16384]{1,0:T(8,128)S(1)}, f32[16,256]{1,0:T(8,128)S(1)}, f32[16,64]{1,0:T(8,128)S(1)}) custom-call(s32[16,64,512]{2,1,0:T(8,128)} %counts_hbm.1, f32[16,512]{1,0:T(8,128)} %nf_hbm.1, f32[16,64]{1,0:T(8,128)} %pf_hbm.1, f32[16,16]{1,0:T(8,128)} %tf_hbm.1), custom_call_target="tpu_custom_call" | custom-call | tf_op jit(solution)/shard_map/gradients/pallas_call | solution.py:312
  38.7 1.0 %store.1 = (f32[16,16384]{1,0:T(8,128)}, f32[16,256]{1,0:T(8,128)}, f32[16,64]{1,0:T(8,128)}) custom-call(f32[16,16384]{1,0:T(8,128)S(1)} %get-tuple-element.6.gn_ref, f32[16,256]{1,0:T(8,128)S(1)} %get-tuple-element.7.gp_ref, f32[16,64]{1,0:T(8,128)S(1)} %get-tuple-element.8.gt_ref), custom_call_target="tpu_custom_call" | custom-call | tf_op jit(solution)/shard_map/store/pallas_call | solution.py:352

commit v4 on v3

--- a/solution.py
+++ b/solution.py
@@ -29,7 +29,7 @@
     nf_ref, pf_ref, tf_ref, counts, stage, proj, part_a, sum_a, part_v, sum_v, mean_v, final,
     a1, a2, v1, v2, v3, other,
     factor_sem, counts_sem, a1_s, a1_r, a2_s, a2_r, a3_s, a3_r, a4_s, a4_r, v1_s, v1_r, v2_s, v2_r, v3_s, v3_r, v4_s, v4_r,
-    plane_sem, cube_sem,
+    plane_sem, cube_sem, link_sem,
 ):
     ranks, i_dev = nf_ref.shape
     j_dev, k_dev = pf_ref.shape[1], tf_ref.shape[1]
@@ -75,14 +75,15 @@
         return (lax.rem(z_, 4) * 4 + x_) * 2 * i_dev
 
     barrier = pltpu.get_barrier_semaphore()
-    greeted = [at(xs_back[a], y, z, core) for a in (1, 2, 3)]
-    greeted += [at(xs_back[a], y, z, 1 - core) for a in range(4)]
-    greeted += [at(x, ys_back[b], z, core) for b in (1, 2, 3)]
-    greeted += [at(x, y, zs_back[c], core) for c in (1, 2, 3)]
-    greeted += [at(x, y, zs[2], core)]
-    greeted += [{"neuron": me, "pos": y, "trial": his_back[h]} for h in (1, 2, 3)]
+    greeted = [at(xs[a], y, z, 0) for a in (1, 2, 3)] + [at(x, ys[b], z, 0) for b in (1, 2, 3)]
+    greeted += [at(x, y, lax.rem(z + 16 + d, 16), 1) for d in (8, 4, -4, 2, -2, 1, -1)]
     for device in greeted:
         pl.semaphore_signal(barrier, inc=1, device_id=device, device_id_type=MESH)
+
+    def greet_core():
+        pl.semaphore_signal(barrier, inc=1, device_id=at(x, y, z, 0), device_id_type=MESH)
+
+    pl.when(core == 1)(greet_core)
 
     for load in factors:
         load.wait()
@@ -139,7 +140,15 @@
     for part in range(i_dev // half):
         part_a[:, pl.ds(part * half, half)] = (acc[part][:ranks] + acc[part][ranks:]) / (positions * trials)
 
-    pl.semaphore_wait(barrier, len(greeted))
+    def hear(count):
+        pl.semaphore_wait(barrier, count)
+        pl.semaphore_signal(link_sem, inc=1, device_id=at(x, y, z, 1 - core), device_id_type=MESH)
+
+    def told():
+        pl.semaphore_wait(link_sem, 1)
+
+    pl.when(core == 0)(lambda: hear(13))
+    pl.when(core == 1)(told)
     for a in (1, 2, 3):
         pl.semaphore_signal(plane_sem, inc=1, device_id=at(xs_back[a], y, z, core), device_id_type=MESH)
 
@@ -187,6 +196,8 @@
     for copy in first_a:
         copy.wait_recv()
     sum_a[...] = (a1[0] + a1[1]) + (a1[2] + quarter_of(part_a, y, 0)[...])
+    pl.when(core == 1)(lambda: hear(14))
+    pl.when(core == 0)(told)
     second_a = [
         send(sum_a, a2.at[h - 1], a2_s.at[h - 1], a2_r.at[h - 1], {"neuron": me, "pos": y, "trial": his[h]})
         for h in (3, 1, 2)
@@ -343,7 +354,7 @@
             dma, dma((16,)), dma((16,)), dma((16,)),
             dma((7,)), dma((7,)), dma((3,)), dma((3,)),
             dma, dma((16,)), dma, dma,
-            pltpu.SemaphoreType.REGULAR, pltpu.SemaphoreType.REGULAR,
+            pltpu.SemaphoreType.REGULAR, pltpu.SemaphoreType.REGULAR, pltpu.SemaphoreType.REGULAR,
         ],
         compiler_params=pltpu.CompilerParams(
             collective_id=0, has_side_effects=True, vmem_limit_bytes=32 << 20

time: 39.9 us -> 38.7 us (0.970)
  Pallas kernels: 39.1 us -> 37.9 us
    pallas_call x1, Pallas kernels: 38.1 us -> 36.9 us  [body(): pl.pallas_call(kernel, name='gradients', out_shape=(pltpu.VMEM((ranks, i_...]
where the time goes in v4:
time: 38.7 us; the launch traced here: 38.5 us
  Pallas kernels  37.9 us (98%)
  between operations  0.64 us (2%)
    pallas_call x1, Pallas kernels, body(): pl.pallas_call(kernel, name='gradients', out_shape=(pltpu.VMEM((ranks, i_...  36.9 us
    pallas_call x1, Pallas kernels, body(): pl.pallas_call(store, name='store', out_shape=tuple((jax.ShapeDtypeStruct...  1.02 us

profile of v4, /device:TPU:1, one launch (start us, length us, event | category | flops | bytes accessed | tf_op | source)
XLA Modules:
  0.0 38.5 jit_solution(12397782229990567526)
XLA Ops:
  0.6 36.9 %gradients.1 = (f32[16,16384]{1,0:T(8,128)S(1)}, f32[16,256]{1,0:T(8,128)S(1)}, f32[16,64]{1,0:T(8,128)S(1)}) custom-call(s32[16,64,512]{2,1,0:T(8,128)} %counts_hbm.1, f32[16,512]{1,0:T(8,128)} %nf_hbm.1, f32[16,64]{1,0:T(8,128)} %pf_hbm.1, f32[16,16]{1,0:T(8,128)} %tf_hbm.1), custom_call_target="tpu_custom_call" | custom-call | tf_op jit(solution)/shard_map/gradients/pallas_call | solution.py:323
  37.5 1.0 %store.1 = (f32[16,16384]{1,0:T(8,128)}, f32[16,256]{1,0:T(8,128)}, f32[16,64]{1,0:T(8,128)}) custom-call(f32[16,16384]{1,0:T(8,128)S(1)} %get-tuple-element.6.gn_ref, f32[16,256]{1,0:T(8,128)S(1)} %get-tuple-element.7.gp_ref, f32[16,64]{1,0:T(8,128)S(1)} %get-tuple-element.8.gt_ref), custom_call_target="tpu_custom_call" | custom-call | tf_op jit(solution)/shard_map/store/pallas_call | solution.py:363

commit v5 on v4

--- a/solution.py
+++ b/solution.py
@@ -228,16 +228,15 @@
     for turn in range(4):
         dz = lax.rem(first + turn, 4) + below
         z_to, c = lax.rem(z + dz + 16, 16), lax.rem(dz + 4, 4)
-        for a in ORDER_X:
-            for b in ORDER_Y:
-
-                def give(a=a, b=b, c=c, z_to=z_to):
-                    send(mine, mine, a3_s, a3_r.at[c * 4 + a], at(xs[a], ys[b], z_to, core))
-
-                if a or b:
-                    give()
-                else:
-                    pl.when(dz != 0)(give)
+        for x_to in (0, 1, 3, 2):
+            dx = lax.rem(x_to - x + 4, 4)
+            a = jnp.where(dx == 2, 3, jnp.where(dx == 3, 2, dx))
+            for y_to in (0, 1, 3, 2):
+
+                def give(a=a, c=c, x_to=x_to, y_to=y_to, z_to=z_to):
+                    send(mine, mine, a3_s, a3_r.at[c * 4 + a], at(x_to, jnp.int32(y_to), z_to, core))
+
+                pl.when((dz != 0) | (x != x_to) | (y != y_to))(give)
         if turn == VTURN:
             for copy in second_v:
                 copy.wait_recv()

time: 38.7 us -> 38.4 us (level)
  no operation moved by 1% of the time
where the time goes in v5:
time: 38.4 us; the launch traced here: 38.2 us
  Pallas kernels  37.6 us (98%)
  between operations  0.64 us (2%)
    pallas_call x1, Pallas kernels, body(): pl.pallas_call(kernel, name='gradients', out_shape=(pltpu.VMEM((ranks, i_...  36.6 us
    pallas_call x1, Pallas kernels, body(): pl.pallas_call(store, name='store', out_shape=tuple((jax.ShapeDtypeStruct...  1.02 us

profile of v5, /device:TPU:1, one launch (start us, length us, event | category | flops | bytes accessed | tf_op | source)
XLA Modules:
  0.0 38.2 jit_solution(7146354074883547874)
XLA Ops:
  0.6 36.6 %gradients.1 = (f32[16,16384]{1,0:T(8,128)S(1)}, f32[16,256]{1,0:T(8,128)S(1)}, f32[16,64]{1,0:T(8,128)S(1)}) custom-call(s32[16,64,512]{2,1,0:T(8,128)} %counts_hbm.1, f32[16,512]{1,0:T(8,128)} %nf_hbm.1, f32[16,64]{1,0:T(8,128)} %pf_hbm.1, f32[16,16]{1,0:T(8,128)} %tf_hbm.1), custom_call_target="tpu_custom_call" | custom-call | tf_op jit(solution)/shard_map/gradients/pallas_call | solution.py:322
  37.2 1.0 %store.1 = (f32[16,16384]{1,0:T(8,128)}, f32[16,256]{1,0:T(8,128)}, f32[16,64]{1,0:T(8,128)}) custom-call(f32[16,16384]{1,0:T(8,128)S(1)} %get-tuple-element.6.gn_ref, f32[16,256]{1,0:T(8,128)S(1)} %get-tuple-element.7.gp_ref, f32[16,64]{1,0:T(8,128)S(1)} %get-tuple-element.8.gt_ref), custom_call_target="tpu_custom_call" | custom-call | tf_op jit(solution)/shard_map/store/pallas_call | solution.py:362
